TPU v7x, 32 devices: a whole 2x2x4 slice. The times are simulated.
32 devices in a mesh: pre: 4 (over x, core), seq: 8 (over z, y).
Axes of the slice: x: 2, y: 2, z: 4, core: 2. Of those that a mesh axis runs over, the one named last changes fastest.
Arguments:
- prefix_in: bfloat16 [8, 512, 2048], P('seq', 'pre'), may hold values from -13 to 13
- later_in: bfloat16 [8, 768, 2048], P('seq', 'pre'), may hold values from -13 to 13
- doc_lengths: int32 [8, 4], P('seq'), may hold values from 1 to 384, 768 in all within a row
- doc_exit: int32 [8, 4], P('seq'), may hold values from 1 to 24
- token_skip: int32 [8, 768], P('seq'), may hold values 0 or 1
- first_gain: bfloat16 [2048], P('seq'), may hold values from 0.5 to 1.5
- first_bias: bfloat16 [2048], P('seq'), may hold values from -1.25 to 1.25
- qkv_weight: bfloat16 [2048, 6144], P('seq'), may hold values from -0.125 to 0.125
- query_bias: bfloat16 [2048], P('seq'), may hold values from -3 to 3
- value_bias: bfloat16 [2048], P('seq'), may hold values from -1.75 to 1.75
- out_weight: bfloat16 [2048, 2048], P('seq'), may hold values from -1 to 1
- out_bias: bfloat16 [2048], P('seq'), may hold values from -1.25 to 1.25
- second_gain: bfloat16 [2048], P('seq'), may hold values from 0.5 to 1.5
- second_bias: bfloat16 [2048], P('seq'), may hold values from -1.25 to 1.25
- up_weight: bfloat16 [2048, 8192], P('seq'), may hold values from -0.125 to 0.125
- up_bias: bfloat16 [8192], P('seq'), may hold values from -1.75 to 1.75
- down_weight: bfloat16 [2048, 8192], P('seq'), may hold values from -0.0625 to 0.0625
- down_bias: bfloat16 [2048], P('seq'), may hold values from -1.25 to 1.25
- prefix_cot: bfloat16 [8, 512, 2048], P('seq', 'pre'), may hold values from -6 to 6
- later_cot: bfloat16 [8, 768, 2048], P('seq', 'pre'), may hold values from -6 to 6
Outputs:
- prefix_out: bfloat16 [8, 512, 2048], P('seq', 'pre')
- later_out: bfloat16 [8, 768, 2048], P('seq', 'pre')
- prefix_grad: bfloat16 [8, 512, 2048], P('seq', 'pre')
- later_grad: bfloat16 [8, 768, 2048], P('seq', 'pre')
- first_gain_grad: float32 [2048], P('seq')
- first_bias_grad: float32 [2048], P('seq')
- qkv_weight_grad: float32 [2048, 6144], P('seq')
- query_bias_grad: float32 [2048], P('seq')
- value_bias_grad: float32 [2048], P('seq')
- out_weight_grad: float32 [2048, 2048], P('seq')
- out_bias_grad: float32 [2048], P('seq')
- second_gain_grad: float32 [2048], P('seq')
- second_bias_grad: float32 [2048], P('seq')
- up_weight_grad: float32 [2048, 8192], P('seq')
- up_bias_grad: float32 [8192], P('seq')
- down_weight_grad: float32 [2048, 8192], P('seq')
- down_bias_grad: float32 [2048], P('seq')
- residual_rms: float32 [3], replicated
Inputs may be any that keep to these rules, and one draw needn't show every extreme that they name: `doc_lengths`: each row's 4 lengths sum to 768; the longest in each row is exactly 384.
All inputs are finite; a program needn't handle non-finite values. No bound on the sum of `token_skip` on one device may be relied on, other than what follows from the above.
Results may differ from a plain program's by a relative error of at most 0.018.
Values may be sent and summed in bfloat16 or wider, within the bound.
A program may use at most 768 MiB of HBM per device.

v0:
```python
from functools import reduce
import math
import jax
import jax.numpy as jnp
from jax import lax
from jax.sharding import PartitionSpec as P

D = 2048
HEADS = 32
HEAD_DIM = 64
FF = 8192
LAYER = 12
PRE = 512
EPS = 1e-05
NEG = -1e30


def layer_norm_parts(values, gain, bias):
    mean = jnp.mean(values, axis=-1, keepdims=True)
    centred = values - mean
    variance = jnp.mean(centred * centred, axis=-1, keepdims=True)
    scaling = lax.rsqrt(variance + EPS)
    normed = centred * scaling
    return (normed * gain + bias, normed, scaling)


def norm_back(grad, normed, scaling, gain):
    scaled = grad * gain
    inner = jnp.mean(scaled, axis=-1, keepdims=True)
    cross = jnp.mean(scaled * normed, axis=-1, keepdims=True)
    return scaling * (scaled - inner - normed * cross)


def gelu_slope(upper):
    cumulative = 0.5 * (1.0 + lax.erf(upper * (1.0 / math.sqrt(2.0))))
    density = jnp.exp(-0.5 * upper * upper) * (1.0 / math.sqrt(2.0 * math.pi))
    return cumulative + upper * density


def token_tables(doc_lengths, doc_exit, token_skip):
    ends = jnp.cumsum(doc_lengths, axis=-1, dtype=jnp.int32)
    starts = ends - doc_lengths
    places = jnp.arange(token_skip.shape[-1], dtype=jnp.int32)
    doc_id = (
        jnp.sum(
            (places[:, None] >= starts[..., None, :]).astype(jnp.int32), axis=-1, dtype=jnp.int32
        )
        - 1
    )
    kinds = jnp.arange(doc_lengths.shape[-1], dtype=jnp.int32)
    live_doc = doc_exit > LAYER
    live = jnp.any((doc_id[..., None] == kinds) & live_doc[..., None, :], axis=-1) & (
        token_skip == 0
    )
    return (doc_id, live)


def split_pairs(pairs):
    rows, count = (pairs.shape[0], pairs.shape[1])
    keys_h = pairs[..., :D].reshape(rows, count, HEADS, HEAD_DIM)
    values_h = pairs[..., D:].reshape(rows, count, HEADS, HEAD_DIM)
    return (keys_h, values_h)


def score_block(queries, keys_h, mask):
    scores = jnp.einsum("bqhd,bkhd->bhqk", queries, keys_h, preferred_element_type=jnp.float32)
    if mask is None:
        return scores
    return jnp.where(mask[:, None], scores, NEG)


def attend(queries, key_sets, masks):
    blocks = [
        score_block(queries, split_pairs(pairs)[0], mask) for pairs, mask in zip(key_sets, masks)
    ]
    top = reduce(jnp.maximum, [jnp.max(block, axis=-1) for block in blocks])
    powers = [jnp.exp(block - top[..., None]) for block in blocks]
    total = reduce(jnp.add, [jnp.sum(power, axis=-1) for power in powers])
    mixed = 0.0
    for power, pairs in zip(powers, key_sets):
        weights = (power / total[..., None]).astype(jnp.bfloat16)
        mixed = mixed + jnp.einsum(
            "bhqk,bkhd->bqhd", weights, split_pairs(pairs)[1], preferred_element_type=jnp.float32
        )
    return (mixed, top, total)


def attend_back(queries, key_sets, masks, top, total, grad_out):
    probs_all = []
    dprob_all = []
    for pairs, mask in zip(key_sets, masks):
        keys_h, values_h = split_pairs(pairs)
        block = score_block(queries, keys_h, mask)
        probs_all.append(jnp.exp(block - top[..., None]) / total[..., None])
        dprob_all.append(
            jnp.einsum("bqhd,bkhd->bhqk", grad_out, values_h, preferred_element_type=jnp.float32)
        )
    delta = reduce(
        jnp.add, [jnp.sum(probs * dprob, axis=-1) for probs, dprob in zip(probs_all, dprob_all)]
    )
    query_grad = 0.0
    parts = []
    for probs, dprob, pairs in zip(probs_all, dprob_all, key_sets):
        score_grad = (probs * (dprob - delta[..., None])).astype(jnp.bfloat16)
        query_grad = query_grad + jnp.einsum(
            "bhqk,bkhd->bqhd", score_grad, split_pairs(pairs)[0], preferred_element_type=jnp.float32
        )
        parts.append((score_grad, probs.astype(jnp.bfloat16)))
    return (query_grad, parts)


def pair_grads(score_grad, weights, queries, grad_out):
    key_grad = jnp.einsum(
        "bhqk,bqhd->bkhd", score_grad, queries, preferred_element_type=jnp.float32
    )
    value_grad = jnp.einsum(
        "bhqk,bqhd->bkhd", weights, grad_out, preferred_element_type=jnp.float32
    )
    count = key_grad.shape[1]
    return jnp.concatenate(
        [key_grad[0].reshape(count, D), value_grad[0].reshape(count, D)], axis=-1
    )


def terms_from(lefts, rights):
    sliced = [part for part in lefts]
    contract = (((0,), (0,)), ((), ()))
    return jnp.concatenate(
        [
            lax.dot_general(left, right, contract, preferred_element_type=jnp.float32)
            for left, right in zip(sliced, rights)
        ],
        axis=1,
    )


def on_device(
    prefix_in,
    later_in,
    doc_lengths,
    doc_exit,
    token_skip,
    first_gain,
    first_bias,
    qkv_weight,
    query_bias,
    value_bias,
    out_weight,
    out_bias,
    second_gain,
    second_bias,
    up_weight,
    up_bias,
    down_weight,
    down_bias,
    prefix_cot,
    later_cot,
):
    scale = 1.0 / math.sqrt(HEAD_DIM)
    pre_part = prefix_in.shape[1]
    later_part = later_in.shape[1]
    seq_count = lax.axis_size("seq")
    pre_count = lax.axis_size("pre")
    seq_place = lax.axis_index("seq")
    pre_place = lax.axis_index("pre")
    tokens = jnp.concatenate([prefix_in[0], later_in[0]], axis=0).astype(jnp.float32)
    (
        full_first_gain,
        full_first_bias,
        full_qkv,
        full_query_bias,
        full_value_bias,
        full_out,
        full_out_bias,
        full_second_gain,
        full_second_bias,
        full_up,
        full_up_bias,
        full_down,
        full_down_bias,
    ) = (
        lax.all_gather(first_gain, "seq", axis=0, tiled=True),
        lax.all_gather(first_bias, "seq", axis=0, tiled=True),
        lax.all_gather(qkv_weight, "seq", axis=0, tiled=True),
        lax.all_gather(query_bias, "seq", axis=0, tiled=True),
        lax.all_gather(value_bias, "seq", axis=0, tiled=True),
        lax.all_gather(out_weight, "seq", axis=0, tiled=True),
        lax.all_gather(out_bias, "seq", axis=0, tiled=True),
        lax.all_gather(second_gain, "seq", axis=0, tiled=True),
        lax.all_gather(second_bias, "seq", axis=0, tiled=True),
        lax.all_gather(up_weight, "seq", axis=0, tiled=True),
        lax.all_gather(up_bias, "seq", axis=0, tiled=True),
        lax.all_gather(down_weight, "seq", axis=0, tiled=True),
        lax.all_gather(down_bias, "seq", axis=0, tiled=True),
    )
    doc_id, live = token_tables(doc_lengths, doc_exit, token_skip)
    start_col = pre_place * later_part
    doc_here = lax.dynamic_slice_in_dim(doc_id, start_col, later_part, 1)
    live_here = lax.dynamic_slice_in_dim(live, start_col, later_part, 1)
    active = jnp.concatenate([jnp.ones((pre_part,), jnp.float32), live_here[0].astype(jnp.float32)])
    later_places = jnp.arange(token_skip.shape[1], dtype=jnp.int32)
    query_places = start_col + jnp.arange(later_part, dtype=jnp.int32)
    later_mask = (
        (later_places[None, :] <= query_places[:, None])
        & (doc_here[0][:, None] == doc_id[0][None, :])
        & live[0][None, :]
    )[None]
    prefix_places = pre_place * pre_part + jnp.arange(pre_part, dtype=jnp.int32)
    prefix_mask = (jnp.arange(PRE, dtype=jnp.int32)[None, :] <= prefix_places[:, None])[None]
    first_out, first_normed, first_scaling = layer_norm_parts(
        tokens, full_first_gain.astype(jnp.float32), full_first_bias.astype(jnp.float32)
    )
    first_h = first_out.astype(jnp.bfloat16)
    projected = jnp.dot(first_h, full_qkv, preferred_element_type=jnp.float32)
    queries = ((projected[:, :D] + full_query_bias.astype(jnp.float32)) * scale).astype(
        jnp.bfloat16
    )
    pairs = jnp.concatenate(
        [projected[:, D : 2 * D], projected[:, 2 * D :] + full_value_bias.astype(jnp.float32)],
        axis=1,
    ).astype(jnp.bfloat16)
    whole_prefix, whole_later = (
        lax.all_gather(pairs[:pre_part], "pre", axis=0, tiled=True),
        lax.all_gather(pairs[pre_part:], "pre", axis=0, tiled=True),
    )
    whole_prefix = whole_prefix[None]
    whole_later = whole_later[None]
    prefix_queries = queries[:pre_part].reshape(1, pre_part, HEADS, HEAD_DIM)
    later_queries = queries[pre_part:].reshape(1, later_part, HEADS, HEAD_DIM)
    prefix_mixed, prefix_top, prefix_total = attend(prefix_queries, [whole_prefix], [prefix_mask])
    later_mixed, later_top, later_total = attend(
        later_queries, [whole_prefix, whole_later], [None, later_mask]
    )
    mixed = jnp.concatenate(
        [prefix_mixed.reshape(pre_part, D), later_mixed.reshape(later_part, D)], axis=0
    ).astype(jnp.bfloat16)
    attn = jnp.dot(mixed, full_out, preferred_element_type=jnp.float32) + full_out_bias.astype(
        jnp.float32
    )
    middle = tokens + attn
    second_out, second_normed, second_scaling = layer_norm_parts(
        middle, full_second_gain.astype(jnp.float32), full_second_bias.astype(jnp.float32)
    )
    second_h = second_out.astype(jnp.bfloat16)
    upper = jnp.dot(second_h, full_up, preferred_element_type=jnp.float32) + full_up_bias.astype(
        jnp.float32
    )
    acted = jax.nn.gelu(upper, approximate=False).astype(jnp.bfloat16)
    ffn = lax.dot_general(
        acted, full_down, (((1,), (1,)), ((), ())), preferred_element_type=jnp.float32
    ) + full_down_bias.astype(jnp.float32)
    result = tokens + active[:, None] * (attn + ffn)
    square_sums = jnp.stack(
        [
            jnp.sum(active * jnp.sum(result * result, axis=-1)),
            jnp.sum(active * jnp.sum(attn * attn, axis=-1)),
            jnp.sum(active * jnp.sum(ffn * ffn, axis=-1)),
            jnp.sum(active),
        ]
    )
    cotangent = jnp.concatenate([prefix_cot[0], later_cot[0]], axis=0).astype(jnp.float32)
    ffn_grad = (active[:, None] * cotangent).astype(jnp.bfloat16)
    full_first_gain, full_qkv, full_out, full_second_gain, full_up, full_down = (
        lax.all_gather(first_gain, "seq", axis=0, tiled=True),
        lax.all_gather(qkv_weight, "seq", axis=0, tiled=True),
        lax.all_gather(out_weight, "seq", axis=0, tiled=True),
        lax.all_gather(second_gain, "seq", axis=0, tiled=True),
        lax.all_gather(up_weight, "seq", axis=0, tiled=True),
        lax.all_gather(down_weight, "seq", axis=0, tiled=True),
    )
    acted_grad = jnp.dot(ffn_grad, full_down, preferred_element_type=jnp.float32)
    upper_grad = (acted_grad * gelu_slope(upper)).astype(jnp.bfloat16)
    second_grad = jnp.dot(upper_grad, full_up.T, preferred_element_type=jnp.float32)
    middle_grad = norm_back(
        second_grad, second_normed, second_scaling, full_second_gain.astype(jnp.float32)
    )
    attn_grad = (active[:, None] * cotangent + middle_grad).astype(jnp.bfloat16)
    mixed_grad = jnp.dot(attn_grad, full_out.T, preferred_element_type=jnp.float32).astype(
        jnp.bfloat16
    )
    prefix_out_grad = mixed_grad[:pre_part].reshape(1, pre_part, HEADS, HEAD_DIM)
    later_out_grad = mixed_grad[pre_part:].reshape(1, later_part, HEADS, HEAD_DIM)
    prefix_query_grad, prefix_parts = attend_back(
        prefix_queries, [whole_prefix], [prefix_mask], prefix_top, prefix_total, prefix_out_grad
    )
    later_query_grad, later_parts = attend_back(
        later_queries,
        [whole_prefix, whole_later],
        [None, later_mask],
        later_top,
        later_total,
        later_out_grad,
    )
    prefix_term = pair_grads(
        prefix_parts[0][0], prefix_parts[0][1], prefix_queries, prefix_out_grad
    ) + pair_grads(later_parts[0][0], later_parts[0][1], later_queries, later_out_grad)
    later_term = pair_grads(later_parts[1][0], later_parts[1][1], later_queries, later_out_grad)
    prefix_pair_grads, later_pair_grads = (
        lax.psum_scatter(
            prefix_term.astype(jnp.bfloat16), "pre", scatter_dimension=0, tiled=True
        ).astype(jnp.float32),
        lax.psum_scatter(
            later_term.astype(jnp.bfloat16), "pre", scatter_dimension=0, tiled=True
        ).astype(jnp.float32),
    )
    rounded_query = jnp.concatenate(
        [prefix_query_grad.reshape(pre_part, D), later_query_grad.reshape(later_part, D)], axis=0
    ).astype(jnp.bfloat16)
    query_grad = (rounded_query.astype(jnp.float32) * scale).astype(jnp.bfloat16)
    pair_grad = jnp.concatenate([prefix_pair_grads, later_pair_grads], axis=0).astype(jnp.bfloat16)
    project_grad = jnp.concatenate([query_grad, pair_grad], axis=1)
    first_grad = jnp.dot(project_grad, full_qkv.T, preferred_element_type=jnp.float32)
    input_grad = (
        cotangent
        + middle_grad
        + norm_back(first_grad, first_normed, first_scaling, full_first_gain.astype(jnp.float32))
    )
    lefts = (first_h, mixed, second_h, ffn_grad)
    rights = (project_grad, attn_grad, upper_grad, acted)
    block_rows = qkv_weight.shape[0] // pre_count
    count_rows = first_h.shape[0]

    def reorder(left):
        return (
            left.reshape(count_rows, seq_count, pre_count, block_rows)
            .transpose(0, 2, 1, 3)
            .reshape(count_rows, D)
        )

    reordered = tuple((reorder(part) for part in lefts))
    own_block = lax.psum_scatter(
        terms_from(reordered, rights), ("pre", "seq"), scatter_dimension=0, tiled=True
    )
    weight_share = lax.all_gather(own_block.astype(jnp.bfloat16), "pre", axis=0, tiled=True).astype(
        own_block.dtype
    )
    totals = lax.psum(
        (
            square_sums,
            jnp.sum(first_grad * first_normed, axis=0),
            jnp.sum(first_grad, axis=0),
            jnp.sum(query_grad.astype(jnp.float32), axis=0),
            jnp.sum(pair_grad[:, D:].astype(jnp.float32), axis=0),
            jnp.sum(attn_grad.astype(jnp.float32), axis=0),
            jnp.sum(second_grad * second_normed, axis=0),
            jnp.sum(second_grad, axis=0),
            jnp.sum(upper_grad.astype(jnp.float32), axis=0),
            jnp.sum(ffn_grad.astype(jnp.float32), axis=0),
        ),
        ("pre", "seq"),
    )

    def own_share(vector):
        width = vector.shape[0] // seq_count
        return lax.dynamic_slice_in_dim(vector, seq_place * width, width, 0)

    residual_rms = jnp.sqrt(totals[0][:3] / (totals[0][3] * D))
    prefix_out = result[:pre_part][None].astype(jnp.bfloat16)
    later_out = result[pre_part:][None].astype(jnp.bfloat16)
    prefix_grad = input_grad[:pre_part][None].astype(jnp.bfloat16)
    later_grad = input_grad[pre_part:][None].astype(jnp.bfloat16)
    return (
        prefix_out,
        later_out,
        prefix_grad,
        later_grad,
        own_share(totals[1]),
        own_share(totals[2]),
        weight_share[:, : 3 * D],
        own_share(totals[3]),
        own_share(totals[4]),
        weight_share[:, 3 * D : 4 * D],
        own_share(totals[5]),
        own_share(totals[6]),
        own_share(totals[7]),
        weight_share[:, 4 * D : 4 * D + FF],
        own_share(totals[8]),
        weight_share[:, 4 * D + FF :],
        own_share(totals[9]),
        residual_rms,
    )


def solution(mesh):
    placed = (
        P("seq", "pre", None),
        P("seq", "pre", None),
        P("seq", None),
        P("seq", None),
        P("seq", None),
        P("seq"),
        P("seq"),
        P("seq", None),
        P("seq"),
        P("seq"),
        P("seq", None),
        P("seq"),
        P("seq"),
        P("seq"),
        P("seq", None),
        P("seq"),
        P("seq", None),
        P("seq"),
        P("seq", "pre", None),
        P("seq", "pre", None),
    )
    return jax.shard_map(
        on_device,
        mesh=mesh,
        in_specs=placed,
        out_specs=(
            P("seq", "pre", None),
            P("seq", "pre", None),
            P("seq", "pre", None),
            P("seq", "pre", None),
            P("seq"),
            P("seq"),
            P("seq", None),
            P("seq"),
            P("seq"),
            P("seq", None),
            P("seq"),
            P("seq"),
            P("seq"),
            P("seq", None),
            P("seq"),
            P("seq", None),
            P("seq"),
            P(),
        ),
        check_vma=False,
    )
```

profile of v0, /device:TPU:0, one launch (start us, length us, event | category | flops | bytes accessed | tf_op | source)
XLA Modules:
  0.0 4279.1 jit_solution(287303370636174228)
XLA Ops:
  10.6 51.4 %all-gather.2 = bf16[8,1,256]{2,1,0:T(2,128)(2,1)S(1)} all-gather(bf16[1,1,256]{2,1,0:T(2,128)(2,1)S(1)} %reshape.627), channel_id=1, replica_groups=mesh['pre'=4,'seq'=8] {'seq'}, dimensions={0}, use_global_device_ids=true | all-gather | bytes 4608 | tf_op jit(solution)/shard_map/all_gather | solution.py:186
  62.0 21.2 all-gather.3
  83.2 29.2 all-gather
  113.0 22.6 all-gather.1
  138.4 354.9 %all-gather.16.cloned.1.call-done = bf16[2048,6144]{1,0:T(8,128)(2,1)} async-done(((bf16[256,6144]{1,0:T(8,128)(2,1)}), bf16[2048,6144]{1,0:T(8,128)(2,1)}) %all-gather.16.cloned.1.call-update) | async-done | bytes 25165840 | tf_op jit(solution)/shard_map/all_gather | solution.py:184
  493.3 12.7 fusion.71
  512.5 19.3 all-gather.6
  531.8 16.3 all-gather.5
  548.1 18.3 all-gather.4
  566.4 26.2 all_gather.66
  605.5 7.5 fusion.103
  613.1 7.5 fusion.102
  623.2 5.4 fusion.100
  641.3 12.6 fusion.4
  658.4 7.9 fusion.26
  666.3 8.4 add_convert_fusion.3
  674.8 44.4 %all-gather.22.cloned.1.call-done = bf16[2048,2048]{1,0:T(8,128)(2,1)} async-done(((bf16[256,2048]{1,0:T(8,128)(2,1)}), bf16[2048,2048]{1,0:T(8,128)(2,1)}) %all-gather.22.cloned.1.call-update) | async-done | bytes 8388624 | tf_op jit(solution)/shard_map/all_gather | solution.py:187
  719.2 8.5 fusion.97
  729.7 626.8 %all-gather.24.cloned.1.call-done = bf16[2048,8192]{1,0:T(8,128)(2,1)} async-done(((bf16[256,8192]{1,0:T(8,128)(2,1)}), bf16[2048,8192]{1,0:T(8,128)(2,1)}) %all-gather.24.cloned.1.call-update) | async-done | bytes 33554448 | tf_op jit(solution)/shard_map/all_gather | solution.py:191
  1356.5 39.7 fusion.8
  1396.2 599.4 %all-gather.26.cloned.1.call-done = bf16[2048,8192]{1,0:T(8,128)(2,1)} async-done(((bf16[256,8192]{1,0:T(8,128)(2,1)}), bf16[2048,8192]{1,0:T(8,128)(2,1)}) %all-gather.26.cloned.1.call-update) | async-done | bytes 33554448 | tf_op jit(solution)/shard_map/all_gather | solution.py:193
  1995.6 23.4 convert_reduce_fusion
  2019.0 20.3 multiply_reduce_fusion.6
  2046.4 6.4 fusion.58
  2052.7 6.7 multiply_reduce_fusion.2
  2059.9 7.8 fusion.30
  2067.7 11.1 multiply_reduce_fusion.1
  2078.8 16.0 multiply_reduce_fusion
  2094.9 6.7 multiply_convert_fusion.2
  2106.0 7.7 multiply_convert_fusion.1
  2122.4 6.4 copy.134
  2128.9 17.0 multiply_convert_fusion
  2153.5 7.9 fusion.55
  2161.4 6.0 pad_maximum_fusion.1
  2167.5 8.6 copy.136
  2198.8 6.9 add_convert_fusion.2
  2210.6 9.7 fusion.107
  2220.3 28.5 fusion.108
  2248.8 28.0 fusion.109
  2282.0 23.0 fusion.62
  2305.0 130.7 %pad_maximum_fusion = f32[2048,24576]{1,0:T(8,128)} fusion(f32[2048,8192]{1,0:T(8,128)} %fusion.109, f32[2048,8192]{1,0:T(8,128)} %fusion.108, f32[2048,2048]{1,0:T(8,128)} %fusion.107, f32[2048,6144]{1,0:T(8,128)} %fusion.62), kind=kLoop, calls=%fused_computation.1 | loop fusion | flops 150994944 | bytes 402653184 | tf_op jit(solution)/shard_map/concatenate | solution.py:128
  2436.3 20.3 all-gather.7
  2456.7 25.8 convolution_add_fusion.1
  2484.7 24.6 fusion.49
  2513.2 1521.3 %reduce-scatter.8.cloned.1.call-done = f32[64,24576]{1,0:T(8,128)} async-done(((f32[2048,24576]{1,0:T(8,128)}), f32[64,24576]{1,0:T(8,128)}) %reduce-scatter.8.cloned.1.call-update) | async-done | bytes 6291472 | tf_op jit(solution)/shard_map/reduce_scatter | solution.py:331
  4048.0 118.9 %all-reduce.4.cloned.1.call-done = (f32[2048]{0:T(1024)}, f32[2048]{0:T(1024)}, f32[2048]{0:T(1024)}, f32[2048]{0:T(1024)}, f32[2048]{0:T(1024)}, /*index=5*/f32...) async-done(((f32[2048]{0:T(1024)}, f32[2048]{0:T(1024)}, f32[2048]{0:T(1024)}, f32[2048]{0:T(1024)}, f32[2048]{0:T(1024)}, ...) | async-done | bytes 98336 | tf_op jit(solution)/shard_map/psum | solution.py:337
  4181.6 70.5 %all-gather.28.cloned.1.call-done = bf16[256,24576]{1,0:T(8,128)(2,1)} async-done(((bf16[64,24576]{1,0:T(8,128)(2,1)}), bf16[256,24576]{1,0:T(8,128)(2,1)}) %all-gather.28.cloned.1.call-update) | async-done | bytes 12582928 | tf_op jit(solution)/shard_map/all_gather | solution.py:334
  4260.2 11.8 fusion.99
  (346 shorter events, 150.7 us)
Async XLA Ops:
  7.2 130.7 %copy-start.12 = (bf16[1,192,2048]{2,1,0:T(8,128)(2,1)S(1)}, bf16[1,192,2048]{2,1,0:T(8,128)(2,1)}, u32[]{:S(2)}) copy-start(bf16[1,192,2048]{2,1,0:T(8,128)(2,1)} %param.21) | copy-start | bytes 2359300
  7.2 130.7 %copy-start.18 = (bf16[1,128,2048]{2,1,0:T(8,128)(2,1)S(1)}, bf16[1,128,2048]{2,1,0:T(8,128)(2,1)}, u32[]{:S(2)}) copy-start(bf16[1,128,2048]{2,1,0:T(8,128)(2,1)} %param.20) | copy-start | bytes 1572868
  7.2 486.1 %all-gather.16.cloned.1.call-start = ((), (), s32[]{:S(2)}) async-start(), calls=%async_computation.3 | async-start | bytes 28311552 | tf_op jit(solution)/shard_map/all_gather | solution.py:184
  7.9 587.8 %all-gather.18.cloned.1.call-start = ((), (), s32[]{:S(2)}) async-start(), calls=%async_computation.4 | async-start | bytes 5242880 | tf_op jit(solution)/shard_map/all_gather | solution.py:223
  113.0 392.9 %copy-start.66 = (f32[8,1,256]{2,1,0:T(1,128)}, f32[8,1,256]{2,1,0:T(1,128)S(1)}, u32[]{:S(2)}) copy-start(f32[8,1,256]{2,1,0:T(1,128)S(1)} %convert_element_type.212) | copy-start | bytes 24580
  137.9 368.1 %copy-start.61 = (f32[320]{0:T(512)}, f32[320]{0:T(512)S(1)}, u32[]{:S(2)}) copy-start(f32[320]{0:T(512)S(1)} %broadcast_multiply_fusion.5) | copy-start | bytes 3844
  138.4 367.6 %copy-start.68 = (f32[320]{0:T(512)}, f32[320]{0:T(512)S(1)}, u32[]{:S(2)}) copy-start(f32[320]{0:T(512)S(1)} %add_rsqrt_fusion.1) | copy-start | bytes 3844
  509.0 114.1 %all-gather.20.cloned.1.call-start = ((), (), s32[]{:S(2)}) async-start(), calls=%async_computation.5 | async-start | bytes 7864320 | tf_op jit(solution)/shard_map/all_gather | solution.py:224
  510.3 208.8 %all-gather.22.cloned.1.call-start = ((), (), s32[]{:S(2)}) async-start(), calls=%async_computation.6 | async-start | bytes 9437184 | tf_op jit(solution)/shard_map/all_gather | solution.py:187
  511.0 55.4 %copy-start.83 = (bf16[1024]{0:T(1024)(128)(2,1)S(1)}, bf16[1024]{0:T(1024)(128)(2,1)}, u32[]{:S(2)}) copy-start(bf16[1024]{0:T(1024)(128)(2,1)} %param.35) | copy-start | bytes 6148
  511.0 81.8 %copy-start.88 = (s32[1,4]{1,0:T(1,128)S(1)}, s32[1,4]{1,0:T(1,128)}, u32[]{:S(2)}) copy-start(s32[1,4]{1,0:T(1,128)} %param.23) | copy-start | bytes 52
  511.0 81.9 %copy-start.82 = (s32[1,768]{1,0:T(1,128)S(1)}, s32[1,768]{1,0:T(1,128)}, u32[]{:S(2)}) copy-start(s32[1,768]{1,0:T(1,128)} %param.24) | copy-start | bytes 9220
  511.0 83.0 %copy-start.31 = (bf16[320,2048]{1,0:T(8,128)(2,1)S(1)}, bf16[320,2048]{1,0:T(8,128)(2,1)}, u32[]{:S(2)}) copy-start(bf16[320,2048]{1,0:T(8,128)(2,1)} %get-tuple-element.55) | copy-start | bytes 3932164
  511.0 845.5 %all-gather.24.cloned.1.call-start = ((), (), s32[]{:S(2)}) async-start(), calls=%async_computation.7 | async-start | bytes 37748736 | tf_op jit(solution)/shard_map/all_gather | solution.py:191
  511.6 1484.0 %all-gather.26.cloned.1.call-start = ((), (), s32[]{:S(2)}) async-start(), calls=%async_computation.8 | async-start | bytes 37748736 | tf_op jit(solution)/shard_map/all_gather | solution.py:193
  512.2 1764.6 %reduce-scatter.10.cloned.1.call-start = ((), (), s32[]{:S(2)}) async-start(), calls=%async_computation.11 | async-start | bytes 5242880
  548.1 1491.2 %copy-start.53 = (f32[8,1,256]{2,1,0:T(1,128)}, f32[8,1,256]{2,1,0:T(1,128)S(1)}, u32[]{:S(2)}) copy-start(f32[8,1,256]{2,1,0:T(1,128)S(1)} %convert_element_type.217) | copy-start | bytes 24580
  594.0 64.4 %copy-start.39 = (pred[192,768]{1,0:T(8,128)(4,1)}, pred[192,768]{1,0:T(8,128)(4,1)S(1)}, u32[]{:S(2)}) copy-start(pred[192,768]{1,0:T(8,128)(4,1)S(1)} %fusion.83) | copy-start | bytes 442372
  641.2 25.1 copy-start.49
  666.3 52.9 %copy-start.13 = (bf16[1,192,2048]{2,1,0:T(8,128)(2,1)S(1)}, bf16[1,192,2048]{2,1,0:T(8,128)(2,1)}, u32[]{:S(2)}) copy-start(bf16[1,192,2048]{2,1,0:T(8,128)(2,1)} %param.21) | copy-start | bytes 2359300
  727.7 1311.6 %copy-start.2 = (f32[320,2048]{1,0:T(8,128)}, f32[320,2048]{1,0:T(8,128)S(1)}, u32[]{:S(2)}) copy-start(f32[320,2048]{1,0:T(8,128)S(1)} %get-tuple-element.50) | copy-start | bytes 7864324
  727.7 1311.6 %copy-start.59 = (f32[320]{0:T(512)}, f32[320]{0:T(512)S(1)}, u32[]{:S(2)}) copy-start(f32[320]{0:T(512)S(1)} %broadcast_multiply_fusion.4) | copy-start | bytes 3844
  728.1 1311.2 %copy-start.64 = (f32[320]{0:T(512)}, f32[320]{0:T(512)S(1)}, u32[]{:S(2)}) copy-start(f32[320]{0:T(512)S(1)} %add_rsqrt_fusion) | copy-start | bytes 3844
  729.7 1265.9 %copy-start.26 = (bf16[1,192,2048]{2,1,0:T(8,128)(2,1)S(1)}, bf16[1,192,2048]{2,1,0:T(8,128)(2,1)}, u32[]{:S(2)}) copy-start(bf16[1,192,2048]{2,1,0:T(8,128)(2,1)} %param.39) | copy-start | bytes 2359300
  729.7 1265.9 %copy-start.75 = (f32[320]{0:T(512)S(1)}, f32[320]{0:T(512)}, u32[]{:S(2)}) copy-start(f32[320]{0:T(512)} %pad_convert_fusion) | copy-start | bytes 3844
  2128.8 149.6 %reduce-scatter.12.cloned.1.call-start = ((), (), s32[]{:S(2)}) async-start(), calls=%async_computation.12 | async-start | bytes 7864320
  2128.8 24.7 slice-start
  2128.9 24.7 slice-start.1
  2128.9 24.6 slice-start.2
  2128.9 24.6 slice-start.3
  2176.2 1858.3 %reduce-scatter.8.cloned.1.call-start = ((), (), s32[]{:S(2)}) async-start(), calls=%async_computation.9 | async-start | bytes 207618048 | tf_op jit(solution)/shard_map/reduce_scatter | solution.py:331
  2220.3 28.5 copy-start.24
  2278.4 26.6 copy-start.21
  2435.7 1731.1 %all-reduce.4.cloned.1.call-start = ((), (), s32[]{:S(2)}) async-start(), calls=%async_computation.13 | async-start | bytes 197632 | tf_op jit(solution)/shard_map/psum | solution.py:337
  2456.7 25.9 copy-start.17
  2456.7 27.9 copy-start.15
  2456.7 27.9 copy-start.20
  2456.7 27.9 copy-start.63
  2456.7 27.9 copy-start.67
  2456.7 27.9 copy-start.70
  2456.7 27.9 copy-start.77
  2513.1 1526.2 %copy-start.3 = (f32[320,2048]{1,0:T(8,128)S(1)}, f32[320,2048]{1,0:T(8,128)}, u32[]{:S(2)}) copy-start(f32[320,2048]{1,0:T(8,128)} %copy-done.2) | copy-start | bytes 7864324
  2513.1 1526.2 %copy-start.54 = (f32[8,1,256]{2,1,0:T(1,128)S(1)}, f32[8,1,256]{2,1,0:T(1,128)}, u32[]{:S(2)}) copy-start(f32[8,1,256]{2,1,0:T(1,128)} %copy-done.53) | copy-start | bytes 24580
  2513.1 1526.2 %copy-start.60 = (f32[320]{0:T(512)S(1)}, f32[320]{0:T(512)}, u32[]{:S(2)}) copy-start(f32[320]{0:T(512)} %copy-done.59) | copy-start | bytes 3844
  2513.2 1526.2 %copy-start.65 = (f32[320]{0:T(512)S(1)}, f32[320]{0:T(512)}, u32[]{:S(2)}) copy-start(f32[320]{0:T(512)} %copy-done.64) | copy-start | bytes 3844
  2513.2 1526.2 %copy-start.72 = (f32[320]{0:T(512)S(1)}, f32[320]{0:T(512)}, u32[]{:S(2)}) copy-start(f32[320]{0:T(512)} %copy-done.71) | copy-start | bytes 3844
  2513.2 1526.2 %copy-start.74 = (f32[320]{0:T(512)S(1)}, f32[320]{0:T(512)}, u32[]{:S(2)}) copy-start(f32[320]{0:T(512)} %copy-done.73) | copy-start | bytes 3844
  2513.2 1738.9 %all-gather.28.cloned.1.call-start = ((), (), s32[]{:S(2)}) async-start(), calls=%async_computation.10 | async-start | bytes 15728640 | tf_op jit(solution)/shard_map/all_gather | solution.py:334
  (63 other events, 446.0 us)
Sparse Core Ops, SparseCore 0:
  9.6 483.6 all-gather.15
  509.1 34.4 all-gather.17
  545.8 46.3 all-gather.19
  594.2 124.9 all-gather.21
  720.5 635.9 all-gather.23
  1357.9 637.6 all-gather.25
  2128.9 44.4 reduce-scatter.9
  2176.7 58.3 reduce-scatter.11
  2435.8 1598.6 reduce-scatter.7
  4041.4 125.3 all-reduce.3
  4169.0 83.0 all-gather.27
where the time goes:
time: 4280 us
  waiting for transfers between devices  3340 us (78%)
  matrix products  361 us (8%)
  blocking collectives  225 us (5%)
  other arithmetic  223 us (5%)
  local copies, waits for them, and re-layouts  115 us (3%)
    reduce_scatter x1, waiting for transfers between devices, on_device(): lax.psum_scatter(terms_from(reordered, rights), ('pre', 'seq'), scatter_d...  1520 us
    all_gather x1, waiting for transfers between devices, on_device(): lax.all_gather(up_weight, 'seq', axis=0, tiled=True)  627 us
    all_gather x1, waiting for transfers between devices, on_device(): lax.all_gather(down_weight, 'seq', axis=0, tiled=True)  599 us
    all_gather x1, waiting for transfers between devices, on_device(): lax.all_gather(qkv_weight, 'seq', axis=0, tiled=True)  355 us
    concatenate x1, other arithmetic, terms_from(): jnp.concatenate([lax.dot_general(left, right, contract, preferred_element...  131 us
    psum x1, waiting for transfers between devices, on_device(): lax.psum((square_sums, jnp.sum(first_grad * first_normed, axis=0), jnp.su...  119 us
    dot_general x4, matrix products, terms_from(): lax.dot_general(left, right, contract, preferred_element_type=jnp.float32)  89.2 us
  transfers between devices with their start and end apart: 11, of which 7 were waited for; matrix products, arithmetic and copies ran while one was open for 9% of the time, Pallas kernels for 0%

commit v1 on v0

--- a/solution.py
+++ b/solution.py
@@ -13,6 +13,19 @@
 PRE = 512
 EPS = 1e-05
 NEG = -1e30
+
+
+def ring_gather(x, axis, dim):
+    ways = lax.axis_size(axis)
+    up = [(d, (d + 1) % ways) for d in range(ways)]
+    down = [(d, (d - 1) % ways) for d in range(ways)]
+    earlier, later = ([x], [x])
+    for _ in range(ways // 2):
+        earlier.append(lax.ppermute(earlier[-1], axis, up))
+    for _ in range((ways - 1) // 2):
+        later.append(lax.ppermute(later[-1], axis, down))
+    line = jnp.concatenate([*earlier[::-1], *later[1:]], axis=dim)
+    return jnp.roll(line, (lax.axis_index(axis) - ways // 2) * x.shape[dim], axis=dim)
 
 
 def layer_norm_parts(values, gain, bias):
@@ -181,7 +194,7 @@
     ) = (
         lax.all_gather(first_gain, "seq", axis=0, tiled=True),
         lax.all_gather(first_bias, "seq", axis=0, tiled=True),
-        lax.all_gather(qkv_weight, "seq", axis=0, tiled=True),
+        ring_gather(qkv_weight, "seq", 0),
         lax.all_gather(query_bias, "seq", axis=0, tiled=True),
         lax.all_gather(value_bias, "seq", axis=0, tiled=True),
         lax.all_gather(out_weight, "seq", axis=0, tiled=True),

time: 4280 us -> 4660 us (1.089)
  waiting for transfers between devices: 3340 us -> 3640 us
  local copies, waits for them, and re-layouts: 115 us -> 166 us
    ppermute x0 -> x7, waiting for transfers between devices: none -> 365 us  [the longest x4 332 us: ring_gather(): earlier.append(lax.ppermute(earlier[-1], axis, up))]
    all_gather x1, waiting for transfers between devices: 355 us -> 234 us  [on_device(): lax.all_gather(qkv_weight, 'seq', axis=0, tiled=True)]
    reduce_scatter x1, waiting for transfers between devices: 1520 us -> 1580 us  [on_device(): lax.psum_scatter(terms_from(reordered, rights), ('pre', 'seq'), scatter_d...]
    unnamed x216 -> x237, local copies, waits for them, and re-layouts: 42.9 us -> 90 us
  transfers between devices with their start and end apart: 11 -> 18, of which waited for: 7 -> 11; matrix products, arithmetic and copies ran while one was open for 9% -> 12% of each run, Pallas kernels for 0% -> 0%
where the time goes in v1:
time: 4660 us; the launch traced here: 4650 us
  waiting for transfers between devices  3640 us (78%)
  matrix products  354 us (8%)
  blocking collectives  234 us (5%)
  other arithmetic  227 us (5%)
  local copies, waits for them, and re-layouts  166 us (4%)
    reduce_scatter x1, waiting for transfers between devices, on_device(): lax.psum_scatter(terms_from(reordered, rights), ('pre', 'seq'), scatter_d...  1580 us
    all_gather x1, waiting for transfers between devices, on_device(): lax.all_gather(up_weight, 'seq', axis=0, tiled=True)  627 us
    all_gather x1, waiting for transfers between devices, on_device(): lax.all_gather(down_weight, 'seq', axis=0, tiled=True)  599 us
    ppermute x4, waiting for transfers between devices, ring_gather(): earlier.append(lax.ppermute(earlier[-1], axis, up))  332 us
    all_gather x1, waiting for transfers between devices, on_device(): lax.all_gather(qkv_weight, 'seq', axis=0, tiled=True)  234 us
    concatenate x1, other arithmetic, terms_from(): jnp.concatenate([lax.dot_general(left, right, contract, preferred_element...  131 us
    psum x1, waiting for transfers between devices, on_device(): lax.psum((square_sums, jnp.sum(first_grad * first_normed, axis=0), jnp.su...  119 us
  transfers between devices with their start and end apart: 18, of which 11 were waited for; matrix products, arithmetic and copies ran while one was open for 12% of the time, Pallas kernels for 0%

profile of v1, /device:TPU:0, one launch (start us, length us, event | category | flops | bytes accessed | tf_op | source)
XLA Modules:
  0.0 4652.7 jit_solution(13447298548455514849)
XLA Ops:
  10.3 71.4 %collective-permute-done = bf16[256,6144]{1,0:T(8,128)(2,1)S(1)} collective-permute-done((bf16[256,6144]{1,0:T(8,128)(2,1)}, bf16[256,6144]{1,0:T(8,128)(2,1)S(1)}, u32[]{:S(2)}, u32[]{:S(2)}) %collective-permute-start) | collective-permute-done | bytes 3145760 | tf_op jit(solution)/shard_map/ppermute | solution.py:24
  86.3 129.8 %collective-permute-done.1 = bf16[256,6144]{1,0:T(8,128)(2,1)S(1)} collective-permute-done((bf16[256,6144]{1,0:T(8,128)(2,1)S(1)}, bf16[256,6144]{1,0:T(8,128)(2,1)S(1)}, u32[]{:S(2)}, u32[]{:S(2)}) %collective-permute-start.1) | collective-permute-done | bytes 3145760 | tf_op jit(solution)/shard_map/ppermute | solution.py:24
  222.5 131.4 %collective-permute-done.2 = bf16[256,6144]{1,0:T(8,128)(2,1)} collective-permute-done((bf16[256,6144]{1,0:T(8,128)(2,1)S(1)}, bf16[256,6144]{1,0:T(8,128)(2,1)}, u32[]{:S(2)}, u32[]{:S(2)}) %collective-permute-start.2) | collective-permute-done | bytes 3145760 | tf_op jit(solution)/shard_map/ppermute | solution.py:24
  359.1 75.9 %all-gather.2 = bf16[8,1,256]{2,1,0:T(2,128)(2,1)S(1)} all-gather(bf16[1,1,256]{2,1,0:T(2,128)(2,1)S(1)} %reshape.627), channel_id=1, replica_groups=mesh['pre'=4,'seq'=8] {'seq'}, dimensions={0}, use_global_device_ids=true | all-gather | bytes 4608 | tf_op jit(solution)/shard_map/all_gather | solution.py:199
  435.0 18.4 all-gather.3
  453.4 16.3 all-gather
  470.3 18.4 all-gather.1
  515.5 32.2 collective-permute-done.6
  573.3 15.3 fusion.1
  599.5 19.4 all-gather.6
  618.9 16.3 all-gather.5
  635.2 18.3 all-gather.4
  653.5 26.2 all_gather.64
  692.6 7.5 fusion.105
  700.2 7.4 fusion.104
  728.4 12.6 fusion.6
  745.6 7.9 fusion.28
  753.5 8.5 add_convert_fusion.3
  761.9 43.7 all-gather.20.cloned.1.call-done
  805.6 8.5 fusion.99
  816.2 626.8 %all-gather.22.cloned.1.call-done = bf16[2048,8192]{1,0:T(8,128)(2,1)} async-done(((bf16[256,8192]{1,0:T(8,128)(2,1)}), bf16[2048,8192]{1,0:T(8,128)(2,1)}) %all-gather.22.cloned.1.call-update) | async-done | bytes 33554448 | tf_op jit(solution)/shard_map/all_gather | solution.py:204
  1443.0 39.7 fusion.10
  1482.7 599.4 %all-gather.24.cloned.1.call-done = bf16[2048,8192]{1,0:T(8,128)(2,1)} async-done(((bf16[256,8192]{1,0:T(8,128)(2,1)}), bf16[2048,8192]{1,0:T(8,128)(2,1)}) %all-gather.24.cloned.1.call-update) | async-done | bytes 33554448 | tf_op jit(solution)/shard_map/all_gather | solution.py:206
  2082.1 23.4 convert_reduce_fusion
  2105.5 20.3 multiply_reduce_fusion.6
  2139.2 6.7 multiply_reduce_fusion.2
  2146.4 7.8 fusion.32
  2154.3 11.1 multiply_reduce_fusion.1
  2165.4 16.0 multiply_reduce_fusion
  2181.4 6.7 multiply_convert_fusion.2
  2192.5 7.7 multiply_convert_fusion.1
  2215.4 17.0 multiply_convert_fusion
  2240.0 7.9 fusion.57
  2254.0 8.6 copy.136
  2285.3 6.9 add_convert_fusion.2
  2297.1 9.7 fusion.109
  2306.8 29.2 fusion.110
  2335.9 28.0 fusion.111
  2369.2 23.1 fusion.64
  2392.2 131.2 %pad_maximum_fusion = f32[2048,24576]{1,0:T(8,128)} fusion(f32[2048,8192]{1,0:T(8,128)} %fusion.111, f32[2048,8192]{1,0:T(8,128)} %fusion.110, f32[2048,2048]{1,0:T(8,128)} %fusion.109, f32[2048,6144]{1,0:T(8,128)} %fusion.64), kind=kLoop, calls=%fused_computation.1 | loop fusion | flops 150994944 | bytes 402653184 | tf_op jit(solution)/shard_map/concatenate | solution.py:141
  2524.1 24.8 all-gather.7
  2548.9 19.2 convolution_add_fusion.1
  2570.1 233.7 %all-gather.26.cloned.1.call-done = bf16[2048,6144]{1,0:T(8,128)(2,1)} async-done(((bf16[256,6144]{1,0:T(8,128)(2,1)}), bf16[2048,6144]{1,0:T(8,128)(2,1)}) %all-gather.26.cloned.1.call-update) | async-done | bytes 25165840 | tf_op jit(solution)/shard_map/all_gather | solution.py:278
  2803.8 20.8 fusion.51
  2828.6 1579.7 %reduce-scatter.8.cloned.1.call-done = f32[64,24576]{1,0:T(8,128)} async-done(((f32[2048,24576]{1,0:T(8,128)}), f32[64,24576]{1,0:T(8,128)}) %reduce-scatter.8.cloned.1.call-update) | async-done | bytes 6291472 | tf_op jit(solution)/shard_map/reduce_scatter | solution.py:344
  4421.7 118.8 %all-reduce.4.cloned.1.call-done = (f32[2048]{0:T(1024)}, f32[2048]{0:T(1024)}, f32[2048]{0:T(1024)}, f32[2048]{0:T(1024)}, f32[2048]{0:T(1024)}, /*index=5*/f32...) async-done(((f32[2048]{0:T(1024)}, f32[2048]{0:T(1024)}, f32[2048]{0:T(1024)}, f32[2048]{0:T(1024)}, f32[2048]{0:T(1024)}, ...) | async-done | bytes 98336 | tf_op jit(solution)/shard_map/psum | solution.py:350
  4555.2 70.5 %all-gather.28.cloned.1.call-done = bf16[256,24576]{1,0:T(8,128)(2,1)} async-done(((bf16[64,24576]{1,0:T(8,128)(2,1)}), bf16[256,24576]{1,0:T(8,128)(2,1)}) %all-gather.28.cloned.1.call-update) | async-done | bytes 12582928 | tf_op jit(solution)/shard_map/all_gather | solution.py:347
  4633.9 11.8 fusion.101
  (382 shorter events, 244.8 us)
Async XLA Ops:
  7.2 675.6 %all-gather.16.cloned.1.call-start = ((), (), s32[]{:S(2)}) async-start(), calls=%async_computation.3 | async-start | bytes 5242880 | tf_op jit(solution)/shard_map/all_gather | solution.py:236
  7.2 74.4 %collective-permute-start = (bf16[256,6144]{1,0:T(8,128)(2,1)}, bf16[256,6144]{1,0:T(8,128)(2,1)S(1)}, u32[]{:S(2)}, u32[]{:S(2)}) collective-permute-start(bf16[256,6144]{1,0:T(8,128)(2,1)} %param.27), channel_id=1, source_target_pairs={{0,1},{1,2},{2,3},{3,4},{4,5},{5,6},{6,7},{7,0},{8,9},{9,10},{10,1... | collective-permute-start | bytes 9437192 | tf_op jit(solution)/shard_map/ppermute | solution.py:24
  81.6 134.5 %collective-permute-start.1 = (bf16[256,6144]{1,0:T(8,128)(2,1)S(1)}, bf16[256,6144]{1,0:T(8,128)(2,1)S(1)}, u32[]{:S(2)}, u32[]{:S(2)}) collective-permute-start(bf16[256,6144]{1,0:T(8,128)(2,1)S(1)} %collective-permute-done), channel_id=1, source_target_pairs={{0,1},{1,2},{2,3},{3,4},{4,5},{5,6},{6,7},{7,0},{8,9},{9,10},{10,1... | collective-permute-start | bytes 9437192 | tf_op jit(solution)/shard_map/ppermute | solution.py:24
  81.6 138.6 %collective-permute-start.4 = (bf16[256,6144]{1,0:T(8,128)(2,1)}, bf16[256,6144]{1,0:T(8,128)(2,1)}, u32[]{:S(2)}, u32[]{:S(2)}) collective-permute-start(bf16[256,6144]{1,0:T(8,128)(2,1)} %param.27), channel_id=1, source_target_pairs={{0,7},{1,0},{2,1},{3,2},{4,3},{5,4},{6,5},{7,6},{8,15},{9,8},{10,9... | collective-permute-start | bytes 9437192 | tf_op jit(solution)/shard_map/ppermute | solution.py:26
  217.8 136.1 %collective-permute-start.2 = (bf16[256,6144]{1,0:T(8,128)(2,1)S(1)}, bf16[256,6144]{1,0:T(8,128)(2,1)}, u32[]{:S(2)}, u32[]{:S(2)}) collective-permute-start(bf16[256,6144]{1,0:T(8,128)(2,1)S(1)} %collective-permute-done.1), channel_id=1, source_target_pairs={{0,1},{1,2},{2,3},{3,4},{4,5},{5,6},{6,7},{7,0},{8,9},{9,10},{10,1... | collective-permute-start | bytes 9437192 | tf_op jit(solution)/shard_map/ppermute | solution.py:24
  220.3 272.4 %collective-permute-start.5 = (bf16[256,6144]{1,0:T(8,128)(2,1)}, bf16[256,6144]{1,0:T(8,128)(2,1)}, u32[]{:S(2)}, u32[]{:S(2)}) collective-permute-start(bf16[256,6144]{1,0:T(8,128)(2,1)} %collective-permute-done.4), channel_id=1, source_target_pairs={{0,7},{1,0},{2,1},{3,2},{4,3},{5,4},{6,5},{7,6},{8,15},{9,8},{10,9... | collective-permute-start | bytes 9437192 | tf_op jit(solution)/shard_map/ppermute | solution.py:26
  353.9 139.0 %collective-permute-start.3 = (bf16[256,6144]{1,0:T(8,128)(2,1)}, bf16[256,6144]{1,0:T(8,128)(2,1)}, u32[]{:S(2)}, u32[]{:S(2)}) collective-permute-start(bf16[256,6144]{1,0:T(8,128)(2,1)} %collective-permute-done.2), channel_id=1, source_target_pairs={{0,1},{1,2},{2,3},{3,4},{4,5},{5,6},{6,7},{7,0},{8,9},{9,10},{10,1... | collective-permute-start | bytes 9437192 | tf_op jit(solution)/shard_map/ppermute | solution.py:24
  470.3 103.0 %copy-start.69 = (f32[8,1,256]{2,1,0:T(1,128)}, f32[8,1,256]{2,1,0:T(1,128)S(1)}, u32[]{:S(2)}) copy-start(f32[8,1,256]{2,1,0:T(1,128)S(1)} %convert_element_type.212) | copy-start | bytes 24580
  490.9 82.4 %copy-start.64 = (f32[320]{0:T(512)}, f32[320]{0:T(512)S(1)}, u32[]{:S(2)}) copy-start(f32[320]{0:T(512)S(1)} %broadcast_multiply_fusion.5) | copy-start | bytes 3844
  492.7 80.6 %copy-start.71 = (f32[320]{0:T(512)}, f32[320]{0:T(512)S(1)}, u32[]{:S(2)}) copy-start(f32[320]{0:T(512)S(1)} %add_rsqrt_fusion.1) | copy-start | bytes 3844
  492.7 55.1 %collective-permute-start.6 = (bf16[256,6144]{1,0:T(8,128)(2,1)}, bf16[256,6144]{1,0:T(8,128)(2,1)S(1)}, u32[]{:S(2)}, u32[]{:S(2)}) collective-permute-start(bf16[256,6144]{1,0:T(8,128)(2,1)} %collective-permute-done.5), channel_id=1, source_target_pairs={{0,7},{1,0},{2,1},{3,2},{4,3},{5,4},{6,5},{7,6},{8,15},{9,8},{10,9... | collective-permute-start | bytes 9437192 | tf_op jit(solution)/shard_map/ppermute | solution.py:26
  595.9 114.3 %all-gather.18.cloned.1.call-start = ((), (), s32[]{:S(2)}) async-start(), calls=%async_computation.4 | async-start | bytes 7864320 | tf_op jit(solution)/shard_map/all_gather | solution.py:237
  597.3 208.4 %all-gather.20.cloned.1.call-start = ((), (), s32[]{:S(2)}) async-start(), calls=%async_computation.5 | async-start | bytes 9437184 | tf_op jit(solution)/shard_map/all_gather | solution.py:200
  598.0 55.5 %copy-start.86 = (bf16[1024]{0:T(1024)(128)(2,1)S(1)}, bf16[1024]{0:T(1024)(128)(2,1)}, u32[]{:S(2)}) copy-start(bf16[1024]{0:T(1024)(128)(2,1)} %param.35) | copy-start | bytes 6148
  598.0 81.9 %copy-start.91 = (s32[1,4]{1,0:T(1,128)S(1)}, s32[1,4]{1,0:T(1,128)}, u32[]{:S(2)}) copy-start(s32[1,4]{1,0:T(1,128)} %param.23) | copy-start | bytes 52
  598.1 82.0 %copy-start.85 = (s32[1,768]{1,0:T(1,128)S(1)}, s32[1,768]{1,0:T(1,128)}, u32[]{:S(2)}) copy-start(s32[1,768]{1,0:T(1,128)} %param.24) | copy-start | bytes 9220
  598.1 83.1 %copy-start.34 = (bf16[320,2048]{1,0:T(8,128)(2,1)S(1)}, bf16[320,2048]{1,0:T(8,128)(2,1)}, u32[]{:S(2)}) copy-start(bf16[320,2048]{1,0:T(8,128)(2,1)} %get-tuple-element.55) | copy-start | bytes 3932164
  598.1 844.9 %all-gather.22.cloned.1.call-start = ((), (), s32[]{:S(2)}) async-start(), calls=%async_computation.6 | async-start | bytes 37748736 | tf_op jit(solution)/shard_map/all_gather | solution.py:204
  598.7 1483.4 %all-gather.24.cloned.1.call-start = ((), (), s32[]{:S(2)}) async-start(), calls=%async_computation.7 | async-start | bytes 37748736 | tf_op jit(solution)/shard_map/all_gather | solution.py:206
  599.2 1764.7 %reduce-scatter.10.cloned.1.call-start = ((), (), s32[]{:S(2)}) async-start(), calls=%async_computation.11 | async-start | bytes 5242880
  635.2 1490.6 %copy-start.56 = (f32[8,1,256]{2,1,0:T(1,128)}, f32[8,1,256]{2,1,0:T(1,128)S(1)}, u32[]{:S(2)}) copy-start(f32[8,1,256]{2,1,0:T(1,128)S(1)} %convert_element_type.217) | copy-start | bytes 24580
  681.1 64.4 %copy-start.42 = (pred[192,768]{1,0:T(8,128)(4,1)}, pred[192,768]{1,0:T(8,128)(4,1)S(1)}, u32[]{:S(2)}) copy-start(pred[192,768]{1,0:T(8,128)(4,1)S(1)} %fusion.84) | copy-start | bytes 442372
  728.4 25.1 copy-start.52
  753.5 52.2 %copy-start.14 = (bf16[1,192,2048]{2,1,0:T(8,128)(2,1)S(1)}, bf16[1,192,2048]{2,1,0:T(8,128)(2,1)}, u32[]{:S(2)}) copy-start(bf16[1,192,2048]{2,1,0:T(8,128)(2,1)} %param.21) | copy-start | bytes 2359300
  814.1 1311.7 %copy-start.2 = (f32[320,2048]{1,0:T(8,128)}, f32[320,2048]{1,0:T(8,128)S(1)}, u32[]{:S(2)}) copy-start(f32[320,2048]{1,0:T(8,128)S(1)} %get-tuple-element.50) | copy-start | bytes 7864324
  814.1 1311.7 %copy-start.62 = (f32[320]{0:T(512)}, f32[320]{0:T(512)S(1)}, u32[]{:S(2)}) copy-start(f32[320]{0:T(512)S(1)} %broadcast_multiply_fusion.4) | copy-start | bytes 3844
  814.6 1311.2 %copy-start.67 = (f32[320]{0:T(512)}, f32[320]{0:T(512)S(1)}, u32[]{:S(2)}) copy-start(f32[320]{0:T(512)S(1)} %add_rsqrt_fusion) | copy-start | bytes 3844
  816.2 1265.9 %copy-start.29 = (bf16[1,192,2048]{2,1,0:T(8,128)(2,1)S(1)}, bf16[1,192,2048]{2,1,0:T(8,128)(2,1)}, u32[]{:S(2)}) copy-start(bf16[1,192,2048]{2,1,0:T(8,128)(2,1)} %param.39) | copy-start | bytes 2359300
  816.2 1265.9 %copy-start.78 = (f32[320]{0:T(512)S(1)}, f32[320]{0:T(512)}, u32[]{:S(2)}) copy-start(f32[320]{0:T(512)} %pad_convert_fusion) | copy-start | bytes 3844
  2215.3 150.3 %reduce-scatter.12.cloned.1.call-start = ((), (), s32[]{:S(2)}) async-start(), calls=%async_computation.12 | async-start | bytes 7864320
  2262.7 541.1 %all-gather.26.cloned.1.call-start = ((), (), s32[]{:S(2)}) async-start(), calls=%async_computation.8 | async-start | bytes 28311552 | tf_op jit(solution)/shard_map/all_gather | solution.py:278
  2263.5 2144.8 %reduce-scatter.8.cloned.1.call-start = ((), (), s32[]{:S(2)}) async-start(), calls=%async_computation.9 | async-start | bytes 207618048 | tf_op jit(solution)/shard_map/reduce_scatter | solution.py:344
  2306.7 29.2 copy-start.27
  2365.6 26.6 copy-start.24
  2523.4 2017.0 %all-reduce.4.cloned.1.call-start = ((), (), s32[]{:S(2)}) async-start(), calls=%async_computation.13 | async-start | bytes 197632 | tf_op jit(solution)/shard_map/psum | solution.py:350
  2548.9 254.9 %copy-start.16 = (bf16[1,192,2048]{2,1,0:T(8,128)(2,1)S(1)}, bf16[1,192,2048]{2,1,0:T(8,128)(2,1)}, u32[]{:S(2)}) copy-start(bf16[1,192,2048]{2,1,0:T(8,128)(2,1)} %param.21) | copy-start | bytes 2359300
  2548.9 254.9 %copy-start.21 = (bf16[1,128,2048]{2,1,0:T(8,128)(2,1)S(1)}, bf16[1,128,2048]{2,1,0:T(8,128)(2,1)}, u32[]{:S(2)}) copy-start(bf16[1,128,2048]{2,1,0:T(8,128)(2,1)} %param.20) | copy-start | bytes 1572868
  2548.9 254.9 %copy-start.66 = (f32[320]{0:T(512)S(1)}, f32[320]{0:T(512)}, u32[]{:S(2)}) copy-start(f32[320]{0:T(512)} %copy-done.64) | copy-start | bytes 3844
  2548.9 254.9 %copy-start.70 = (f32[8,1,256]{2,1,0:T(1,128)S(1)}, f32[8,1,256]{2,1,0:T(1,128)}, u32[]{:S(2)}) copy-start(f32[8,1,256]{2,1,0:T(1,128)} %copy-done.69) | copy-start | bytes 24580
  2548.9 254.9 %copy-start.73 = (f32[320]{0:T(512)S(1)}, f32[320]{0:T(512)}, u32[]{:S(2)}) copy-start(f32[320]{0:T(512)} %copy-done.71) | copy-start | bytes 3844
  2548.9 254.9 %copy-start.80 = (f32[320]{0:T(512)S(1)}, f32[320]{0:T(512)}, u32[]{:S(2)}) copy-start(f32[320]{0:T(512)} %pad_convert_fusion) | copy-start | bytes 3844
  2828.5 1584.6 %copy-start.3 = (f32[320,2048]{1,0:T(8,128)S(1)}, f32[320,2048]{1,0:T(8,128)}, u32[]{:S(2)}) copy-start(f32[320,2048]{1,0:T(8,128)} %copy-done.2) | copy-start | bytes 7864324
  2828.5 1584.6 %copy-start.57 = (f32[8,1,256]{2,1,0:T(1,128)S(1)}, f32[8,1,256]{2,1,0:T(1,128)}, u32[]{:S(2)}) copy-start(f32[8,1,256]{2,1,0:T(1,128)} %copy-done.56) | copy-start | bytes 24580
  2828.5 1584.6 %copy-start.63 = (f32[320]{0:T(512)S(1)}, f32[320]{0:T(512)}, u32[]{:S(2)}) copy-start(f32[320]{0:T(512)} %copy-done.62) | copy-start | bytes 3844
  2828.5 1584.6 %copy-start.68 = (f32[320]{0:T(512)S(1)}, f32[320]{0:T(512)}, u32[]{:S(2)}) copy-start(f32[320]{0:T(512)} %copy-done.67) | copy-start | bytes 3844
  2828.5 1584.6 %copy-start.75 = (f32[320]{0:T(512)S(1)}, f32[320]{0:T(512)}, u32[]{:S(2)}) copy-start(f32[320]{0:T(512)} %copy-done.74) | copy-start | bytes 3844
  2828.5 1584.6 %copy-start.77 = (f32[320]{0:T(512)S(1)}, f32[320]{0:T(512)}, u32[]{:S(2)}) copy-start(f32[320]{0:T(512)} %copy-done.76) | copy-start | bytes 3844
  2828.5 1797.2 %all-gather.28.cloned.1.call-start = ((), (), s32[]{:S(2)}) async-start(), calls=%async_computation.10 | async-start | bytes 15728640 | tf_op jit(solution)/shard_map/all_gather | solution.py:347
  (73 other events, 573.0 us)
Sparse Core Ops, SparseCore 0:
  596.0 33.8 all-gather.15
  632.1 46.3 all-gather.17
  680.7 124.9 all-gather.19
  807.0 635.8 all-gather.21
  1444.3 637.6 all-gather.23
  2215.4 44.4 reduce-scatter.9
  2263.2 58.3 reduce-scatter.11
  2323.1 480.5 all-gather.25
  2810.2 1598.0 reduce-scatter.7
  4415.1 125.2 all-reduce.3
  4542.7 83.0 all-gather.27
